TPU v7x, 32 devices: a whole 2x2x4 slice. The times are simulated.
32 devices in a mesh: dp: 4 (over y, core), expert: 8 (over z, x).
Axes of the slice: x: 2, y: 2, z: 4, core: 2. Of those that a mesh axis runs over, the one named last changes fastest.
Arguments:
- tokens: bfloat16 [4096, 2048], P(('dp', 'expert')), may hold values from -6 to 6
- cotangent: bfloat16 [4096, 2048], P(('dp', 'expert')), may hold values from -6 to 6
- hot_mask: int32 [4096], P(('dp', 'expert')), may hold values 0 or 1
- hot_gate: float32 [4096], P(('dp', 'expert')), may hold values from 0.2 to 1
- cold_ids: int32 [4096, 1], P(('dp', 'expert')), may hold values from 0 to 3; in each aligned block of 128 rows (0 to 127, 128 to 255, ...) at most 40 rows name the same one
- cold_gate: float32 [4096, 1], P(('dp', 'expert')), may hold values from 0.2 to 1
- hot_in: bfloat16 [2, 704, 2048], P(None, 'dp'), may hold values from -0.125 to 0.125
- hot_down: bfloat16 [704, 2048], P('dp'), may hold values from -0.21875 to 0.21875
- cold_in: bfloat16 [2, 2816, 2048], P(None, 'expert'), may hold values from -0.125 to 0.125
- cold_down: bfloat16 [2816, 2048], P('expert'), may hold values from -0.21875 to 0.21875
Outputs:
- mixed: bfloat16 [4096, 2048], P(('dp', 'expert'))
- input_grad: bfloat16 [4096, 2048], P(('dp', 'expert'))
- hot_grad_in: float32 [2, 704, 2048], P(None, 'dp', 'expert')
- hot_grad_down: float32 [704, 2048], P('dp', 'expert')
- cold_grad_in: bfloat16 [4, 2, 2816, 2048], P('dp', None, 'expert')
- cold_grad_down: bfloat16 [4, 2816, 2048], P('dp', 'expert')
Inputs may be any that keep to these rules, and one draw needn't show every extreme that they name: `cold_ids`: in each device's block of 128 rows no cold expert is chosen by more than 40 rows, and in every draw some device's block chooses some cold expert exactly 40 times.
All inputs are finite; a program needn't handle non-finite values. No bound on the sum of `hot_mask` on one device may be relied on, other than what follows from the above.
Results may differ from a plain program's by a relative error of at most 0.0059.
Values may be sent and summed in bfloat16 or wider, within the bound.
A program may use at most 128 MiB of HBM per device.

v0:
```python
import math

import jax
import jax.numpy as jnp
from jax import lax
from jax.sharding import PartitionSpec as P


def silu_parts(values):
    sigmoid_val = jax.nn.sigmoid(values)
    return (values * sigmoid_val, sigmoid_val * (1.0 + values * (1.0 - sigmoid_val)))


def hot_terms(tokens, cotangent, hot_weight, weights):
    pre_act = jnp.einsum("td,kud->ktu", tokens, weights[:2], preferred_element_type=jnp.float32)
    silu_out, silu_slope = silu_parts(pre_act[0])
    hidden = (hot_weight[:, None] * silu_out * pre_act[1]).astype(jnp.bfloat16)
    out_part = jnp.dot(hidden, weights[2], preferred_element_type=jnp.float32)
    back_proj = jnp.einsum("td,ud->tu", cotangent, weights[2], preferred_element_type=jnp.float32)
    hidden_grad = hot_weight[:, None] * back_proj
    pre_grad = jnp.stack([hidden_grad * pre_act[1] * silu_slope, hidden_grad * silu_out]).astype(
        jnp.bfloat16
    )
    dx_part = jnp.einsum("ktu,kud->td", pre_grad, weights[:2], preferred_element_type=jnp.float32)
    grad_in = jnp.einsum("ktu,td->kud", pre_grad, tokens, preferred_element_type=jnp.float32)
    grad_down = jnp.einsum("tu,td->ud", hidden, cotangent, preferred_element_type=jnp.float32)
    return (out_part, dx_part, jnp.concatenate([grad_in, grad_down[None]], axis=0))


def cold_terms(row_block, cold_in, cold_down):
    pre_act = jnp.einsum("rd,kud->kru", row_block[0], cold_in, preferred_element_type=jnp.float32)
    silu_out, silu_slope = silu_parts(pre_act[0])
    hidden = (silu_out * pre_act[1]).astype(jnp.bfloat16)
    out_part = jnp.dot(hidden, cold_down, preferred_element_type=jnp.float32).astype(jnp.bfloat16)
    back_proj = jnp.einsum("rd,ud->ru", row_block[1], cold_down, preferred_element_type=jnp.float32)
    pre_grad = jnp.stack([back_proj * pre_act[1] * silu_slope, back_proj * silu_out]).astype(
        jnp.bfloat16
    )
    dx_part = jnp.einsum(
        "kru,kud->rd", pre_grad, cold_in, preferred_element_type=jnp.float32
    ).astype(jnp.bfloat16)
    grad_in = jnp.einsum("kru,rd->kud", pre_grad, row_block[0], preferred_element_type=jnp.float32)
    grad_down = jnp.einsum("ru,rd->ud", hidden, row_block[1], preferred_element_type=jnp.float32)
    return (out_part, dx_part, grad_in, grad_down)


def body(
    tokens, cotangent, hot_mask, hot_gate, cold_ids, cold_gate, hot_in, hot_down, cold_in, cold_down
):
    tok_dev, model_width = tokens.shape
    top_cold = cold_ids.shape[1]
    data_count = lax.axis_size("dp")
    owner_count = lax.axis_size("expert")
    cold_count = owner_count // 2
    capacity = 5 * tok_dev * top_cold // (4 * cold_count)
    hot_weight = hot_mask.astype(jnp.float32) * hot_gate
    hot_stack = jnp.concatenate([hot_in, hot_down[None]], axis=0)
    ids_flat = cold_ids.reshape(-1)
    one_hot = (ids_flat[:, None] == jnp.arange(cold_count, dtype=jnp.int32)[None, :]).astype(
        jnp.int32
    )
    earlier = jnp.cumsum(one_hot, axis=0) - one_hot
    slot_pos = jnp.sum(one_hot * earlier, axis=1)
    column = ids_flat * capacity + slot_pos
    dispatch = (
        column[:, None] == jnp.arange(cold_count * capacity, dtype=jnp.int32)[None, :]
    ).astype(jnp.bfloat16)
    gates_flat = cold_gate.reshape(-1)
    row_tok = jnp.repeat(tokens, top_cold, axis=0)
    row_cot = (gates_flat[:, None] * jnp.repeat(cotangent, top_cold, axis=0)).astype(jnp.bfloat16)
    stacked = jnp.stack([row_tok, row_cot])
    send_rows = jnp.einsum(
        "rc,srd->scd", dispatch, stacked, preferred_element_type=jnp.float32
    ).astype(jnp.bfloat16)
    send_rows = send_rows.reshape(2, cold_count, capacity, model_width)
    duplicate = jnp.broadcast_to(
        send_rows[:, :, None], (2, cold_count, 2, capacity, model_width)
    ).reshape(2, owner_count, capacity, model_width)
    received = lax.all_to_all(duplicate, "expert", split_axis=1, concat_axis=1, tiled=True)
    row_block = received.reshape(2, owner_count * capacity, model_width)
    out_part, dx_part, cold_grad_in, cold_grad_down = cold_terms(row_block, cold_in, cold_down)
    returned = lax.all_to_all(
        jnp.stack([out_part, dx_part]).reshape(2, owner_count, capacity, model_width),
        "expert",
        split_axis=1,
        concat_axis=1,
        tiled=True,
    )
    summed = jnp.sum(
        returned.astype(jnp.float32).reshape(2, cold_count, 2, capacity, model_width), axis=2
    )
    summed = summed.reshape(2, cold_count * capacity, model_width)
    picked = jnp.take(summed, column, axis=1)
    cold_out = jnp.sum(
        gates_flat.reshape(tok_dev, top_cold, 1)
        * picked[0].reshape(tok_dev, top_cold, model_width),
        axis=1,
    )
    cold_dx = jnp.sum(picked[1].reshape(tok_dev, top_cold, model_width), axis=1)
    full_stack = lax.all_gather(hot_stack, "dp", axis=1, tiled=True)
    hot_out, hot_dx, full_grads = hot_terms(tokens, cotangent, hot_weight, full_stack)
    hot_grads = lax.psum_scatter(full_grads, "dp", scatter_dimension=1, tiled=True)
    scale_hot = 1.0 / math.sqrt(tok_dev * data_count * owner_count)
    hot_cols = lax.psum_scatter(hot_grads, "expert", scatter_dimension=2, tiled=True) * scale_hot
    scale_cold = 1.0 / math.sqrt(tok_dev * owner_count)
    mixed = (hot_out + cold_out).astype(jnp.bfloat16)
    input_grad = (hot_dx + cold_dx).astype(jnp.bfloat16)
    return (
        mixed,
        input_grad,
        hot_cols[:2],
        hot_cols[2],
        (cold_grad_in * scale_cold).astype(jnp.bfloat16)[None],
        (cold_grad_down * scale_cold).astype(jnp.bfloat16)[None],
    )


def solution(mesh):
    return jax.shard_map(
        body,
        mesh=mesh,
        in_specs=(
            P(("dp", "expert"), None),
            P(("dp", "expert"), None),
            P(("dp", "expert")),
            P(("dp", "expert")),
            P(("dp", "expert"), None),
            P(("dp", "expert"), None),
            P(None, "dp", None),
            P("dp", None),
            P(None, "expert", None),
            P("expert", None),
        ),
        out_specs=(
            P(("dp", "expert"), None),
            P(("dp", "expert"), None),
            P(None, "dp", "expert"),
            P("dp", "expert"),
            P("dp", None, "expert", None),
            P("dp", "expert", None),
        ),
        check_vma=False,
    )
```

profile of v0, /device:TPU:0, one launch (start us, length us, event | category | flops | bytes accessed | tf_op | source)
XLA Modules:
  0.0 369.1 jit_solution(3343457779531298084)
XLA Ops:
  7.2 0.0 copy-start
  7.2 0.0 all-gather.2.cloned.1.call-start
  7.3 3.3 pad_maximum_fusion.2
  10.5 0.0 all-gather.2.cloned.1.call-update
  10.5 0.0 reduce-scatter.3.cloned.1.call-start
  10.6 62.6 %all-gather.2.cloned.1.call-done = bf16[3,704,2048]{2,1,0:T(8,128)(2,1)} async-done(((bf16[3,176,2048]{2,1,0:T(8,128)(2,1)}), bf16[3,704,2048]{2,1,0:T(8,128)(2,1)}) %all-gather.2.cloned.1.call-update) | async-done | bytes 8650768 | tf_op jit(solution)/shard_map/all_gather | solution.py:100
  73.2 4.5 %convolution_bitcast_fusion.3 = f32[2,128,704]{1,2,0:T(8,128)S(1)} fusion(bf16[3,704,2048]{2,1,0:T(8,128)(2,1)} %all-gather.2.cloned.1.call-done, bf16[128,2048]{1,0:T(8,128)(2,1)S(1)} %copy-done.1), kind=kOutput, calls=%fused_computation.28 | convolution fusion | flops 738197504 | bytes 9895936 | tf_op jit(solution)/shard_map/td,kud->ktu/dot_general | solution.py:15
  77.7 0.9 convolution_bitcast_fusion
  78.6 1.0 fusion.55
  79.6 0.0 copy-start.8
  79.6 0.7 copy-done.8
  80.3 0.1 copy-done.10
  80.3 1.6 fusion.27
  82.0 6.3 %pad_maximum_fusion = f32[3,704,2048]{2,1,0:T(8,128)} fusion(f32[1,704,2048]{2,1,0:T(8,128)S(1)} %convolution_bitcast_fusion, f32[2,704,2048]{2,1,0:T(8,128)S(1)} %fusion.27), kind=kLoop, calls=%fused_computation.1 | loop fusion | flops 4325376 | bytes 34603008 | tf_op jit(solution)/shard_map/concatenate | solution.py:27
  88.3 0.0 reduce-scatter.3.cloned.1.call-update
  88.3 0.6 copy-done.12
  88.9 0.1 fusion.58
  89.0 0.2 reduce_window_sum.11
  89.2 0.2 select_reduce_fusion
  89.4 1.2 fusion.26
  90.6 0.5 convolution_convert_fusion.1
  91.1 0.1 copy.17
  91.2 1.8 broadcast_in_dim.37
  93.0 5.5 %all-to-all-start = ((bf16[2,8,40,2048]{3,2,0,1:T(8,128)(2,1)}), bf16[2,8,40,2048]{3,2,0,1:T(8,128)(2,1)}, u32[]{:S(2)}, u32[]{:S(2)}) async-start(bf16[2,8,40,2048]{3,2,0,1:T(8,128)(2,1)} %bitcast.201), calls=%async_computation | async-start | bytes 5242880 | tf_op jit(solution)/shard_map/all_to_all | solution.py:79
  98.5 0.0 reduce-scatter.5.cloned.1.call-start
  98.5 119.2 %reduce-scatter.3.cloned.1.call-done = f32[3,176,2048]{2,1,0:T(8,128)} async-done(((f32[3,704,2048]{2,1,0:T(8,128)}), f32[3,176,2048]{2,1,0:T(8,128)}) %reduce-scatter.3.cloned.1.call-update) | async-done | bytes 4325392 | tf_op jit(solution)/shard_map/reduce_scatter | solution.py:102
  217.7 0.0 reduce-scatter.5.cloned.1.call-update
  217.7 1.9 fusion.71
  219.7 1.3 convolution_bitcast_fusion.2
  221.0 1.0 copy-done.15
  222.0 0.9 convolution_convert_fusion
  222.9 0.9 fusion.49
  223.8 1.2 fusion.4
  225.0 1.8 pad_maximum_fusion.1
  226.8 5.5 %all-to-all-start.1 = ((bf16[2,8,40,2048]{3,2,0,1:T(8,128)(2,1)}), bf16[2,8,40,2048]{3,2,0,1:T(8,128)(2,1)}, u32[]{:S(2)}, u32[]{:S(2)}) async-start(bf16[2,8,40,2048]{3,2,0,1:T(8,128)(2,1)} %pad_maximum_fusion.1), calls=%async_computation.1 | async-start | bytes 5242880 | tf_op jit(solution)/shard_map/all_to_all | solution.py:82
  232.3 3.8 %fusion.5 = bf16[1,352,2048]{2,1,0:T(8,128)(2,1)} fusion(bf16[320,2048]{1,0:T(8,128)(2,1)} %bitcast.208, f32[2,320,352]{2,1,0:T(8,128)} %copy-done.18), kind=kOutput, calls=%fused_computation.16 | convolution fusion | flops 463491072 | bytes 3653632 | tf_op jit(solution)/shard_map/ru,rd->ud/dot_general | solution.py:43
  236.1 3.3 fusion.2
  239.4 83.6 %all-to-all-done.1 = bf16[2,8,40,2048]{3,2,0,1:T(8,128)(2,1)} async-done(((bf16[2,8,40,2048]{3,2,0,1:T(8,128)(2,1)}), bf16[2,8,40,2048]{3,2,0,1:T(8,128)(2,1)}, u32[]{:S(2)}, u32[]{:S(2)}) %all-to-all-start.1) | async-done | bytes 2621472 | tf_op jit(solution)/shard_map/all_to_all | solution.py:82
  323.0 2.7 convert_reduce_fusion
  325.7 3.5 copy.21
  329.3 5.7 %gather_fusion = f32[128,2,2048]{2,1,0:T(2,128)} fusion(f32[2,160,2048]{2,0,1:T(2,128)} %bitcast.202, s32[1024]{0:T(1024)S(1)} %pad_clamp_fusion), kind=kCustom, calls=%fused_computation | custom fusion | bytes 4194816 | tf_op jit(solution)/shard_map/jit(_take)/gather | solution.py:93
  335.0 3.0 fusion.19
  338.1 3.7 fusion.15
  341.7 4.5 %fusion.16 = bf16[128,2048]{1,0:T(8,128)(2,1)} fusion(bf16[3,704,2048]{2,1,0:T(8,128)(2,1)} %all-gather.2.cloned.1.call-done, f32[2,128,2048]{2,1,0:T(8,128)S(1)} %fusion.19, bf16[1,128,704]{1,2,0:T(8,128)(2,1)S(1)} %copy-done.11, bf16[1,128,704]{1,2,0:T(8,128)(2,1)S(1)} %copy-done.9), kind=kOutput, calls=%fused_computation.23 | convolution fusion | flops 738902016 | bytes 7700480 | tf_op jit(solution)/shard_map/ktu,kud->td/dot_general | solution.py:24
  346.2 13.8 %reduce-scatter.5.cloned.1.call-done = f32[3,176,256]{2,1,0:T(8,128)} async-done(((f32[3,176,2048]{2,1,0:T(8,128)}), f32[3,176,256]{2,1,0:T(8,128)}) %reduce-scatter.5.cloned.1.call-update) | async-done | bytes 540688 | tf_op jit(solution)/shard_map/reduce_scatter | solution.py:104
  360.0 1.1 broadcast_multiply_fusion
  361.1 0.8 slice.68
  361.9 0.7 slice_bitcast_fusion.13
  (37 shorter events, 0.1 us)
Async XLA Ops:
  7.2 212.5 %copy-start = (bf16[2,352,2048]{2,1,0:T(8,128)(2,1)S(1)}, bf16[2,352,2048]{2,1,0:T(8,128)(2,1)}, u32[]{:S(2)}) copy-start(bf16[2,352,2048]{2,1,0:T(8,128)(2,1)} %param.18) | copy-start | bytes 8650756
  7.2 66.0 %all-gather.2.cloned.1.call-start = ((), (), s32[]{:S(2)}) async-start(), calls=%async_computation.4 | async-start | bytes 10813440 | tf_op jit(solution)/shard_map/all_gather | solution.py:100
  7.2 3.4 copy-start.16
  7.2 3.4 copy-start.17
  7.2 65.9 %copy-start.1 = (bf16[128,2048]{1,0:T(8,128)(2,1)S(1)}, bf16[128,2048]{1,0:T(8,128)(2,1)}, u32[]{:S(2)}) copy-start(bf16[128,2048]{1,0:T(8,128)(2,1)} %param.10) | copy-start | bytes 1572868
  10.5 207.2 %reduce-scatter.3.cloned.1.call-start = ((), (), s32[]{:S(2)}) async-start(), calls=%async_computation.5 | async-start | bytes 21626880 | tf_op jit(solution)/shard_map/reduce_scatter | solution.py:102
  73.2 4.5 %copy-start.2 = (bf16[128,2048]{1,0:T(8,128)(2,1)S(1)}, bf16[128,2048]{1,0:T(8,128)(2,1)}, u32[]{:S(2)}) copy-start(bf16[128,2048]{1,0:T(8,128)(2,1)} %param.11) | copy-start | bytes 1572868
  73.2 5.4 %copy-start.14 = (bf16[3,704,2048]{2,1,0:T(8,128)(2,1)S(1)}, bf16[3,704,2048]{2,1,0:T(8,128)(2,1)}, u32[]{:S(2)}) copy-start(bf16[3,704,2048]{2,1,0:T(8,128)(2,1)} %all-gather.2.cloned.1.call-done) | copy-start | bytes 25952260
  77.7 0.9 copy-start.6
  79.6 0.7 copy-start.8
  79.6 0.7 copy-start.10
  88.2 0.7 copy-start.12
  88.2 1.1 copy-start.13
  93.0 124.8 %all-to-all-start = ((bf16[2,8,40,2048]{3,2,0,1:T(8,128)(2,1)}), bf16[2,8,40,2048]{3,2,0,1:T(8,128)(2,1)}, u32[]{:S(2)}, u32[]{:S(2)}) async-start(bf16[2,8,40,2048]{3,2,0,1:T(8,128)(2,1)} %bitcast.201), calls=%async_computation | async-start | bytes 5242880 | tf_op jit(solution)/shard_map/all_to_all | solution.py:79
  98.5 261.6 %reduce-scatter.5.cloned.1.call-start = ((), (), s32[]{:S(2)}) async-start(), calls=%async_computation.6 | async-start | bytes 4866048 | tf_op jit(solution)/shard_map/reduce_scatter | solution.py:104
  219.6 1.3 copy-start.3
  219.7 3.2 copy-start.5
  219.7 2.3 copy-start.15
  222.0 1.8 copy-start.18
  226.8 96.2 %all-to-all-start.1 = ((bf16[2,8,40,2048]{3,2,0,1:T(8,128)(2,1)}), bf16[2,8,40,2048]{3,2,0,1:T(8,128)(2,1)}, u32[]{:S(2)}, u32[]{:S(2)}) async-start(bf16[2,8,40,2048]{3,2,0,1:T(8,128)(2,1)} %pad_maximum_fusion.1), calls=%async_computation.1 | async-start | bytes 5242880 | tf_op jit(solution)/shard_map/all_to_all | solution.py:82
  232.3 3.8 %copy-start.4 = (bf16[1,8,40,2048]{3,2,0,1:T(8,128)(2,1)S(1)}, bf16[1,8,40,2048]{3,2,0,1:T(8,128)(2,1)}, u32[]{:S(2)}) copy-start(bf16[1,8,40,2048]{3,2,0,1:T(8,128)(2,1)} %copy-done.3) | copy-start | bytes 3932164
  335.0 3.0 copy-start.7
  338.0 3.7 %copy-start.9 = (bf16[1,128,704]{1,2,0:T(8,128)(2,1)S(1)}, bf16[1,128,704]{1,2,0:T(8,128)(2,1)}, u32[]{:S(2)}) copy-start(bf16[1,128,704]{1,2,0:T(8,128)(2,1)} %copy-done.8) | copy-start | bytes 540676
  338.0 3.7 %copy-start.11 = (bf16[1,128,704]{1,2,0:T(8,128)(2,1)S(1)}, bf16[1,128,704]{1,2,0:T(8,128)(2,1)}, u32[]{:S(2)}) copy-start(bf16[1,128,704]{1,2,0:T(8,128)(2,1)} %copy-done.10) | copy-start | bytes 540676
Sparse Core Ops, SparseCore 0:
  10.7 62.4 all-gather.1
  88.4 129.2 reduce-scatter.2
  221.8 138.2 reduce-scatter.4
where the time goes:
time: 370 us; the launch traced here: 369 us
  waiting for transfers between devices  279 us (75%)
  matrix products  28 us (8%)
  other arithmetic  19.8 us (5%)
  local copies, waits for them, and re-layouts  16.9 us (5%)
  between operations  14.1 us (4%)
  starting transfers between devices  11.1 us (3%)
    reduce_scatter x1, waiting for transfers between devices, body(): lax.psum_scatter(full_grads, 'dp', scatter_dimension=1, tiled=True)  119 us
    all_to_all x1, waiting for transfers between devices, body(): lax.all_to_all(jnp.stack([out_part, dx_part]).reshape(2, owner_count, cap...  83.6 us
    all_gather x1, waiting for transfers between devices, body(): full_stack = lax.all_gather(hot_stack, 'dp', axis=1, tiled=True)  62.6 us
    reduce_scatter x1, waiting for transfers between devices, body(): lax.psum_scatter(hot_grads, 'expert', scatter_dimension=2, tiled=True)  13.8 us
  transfers between devices with their start and end apart: 5, of which 4 were waited for; matrix products, arithmetic and copies ran while one was open for 11% of the time, Pallas kernels for 0%

commit v1 on v0

--- a/solution.py
+++ b/solution.py
@@ -22,9 +22,7 @@
         jnp.bfloat16
     )
     dx_part = jnp.einsum("ktu,kud->td", pre_grad, weights[:2], preferred_element_type=jnp.float32)
-    grad_in = jnp.einsum("ktu,td->kud", pre_grad, tokens, preferred_element_type=jnp.float32)
-    grad_down = jnp.einsum("tu,td->ud", hidden, cotangent, preferred_element_type=jnp.float32)
-    return (out_part, dx_part, jnp.concatenate([grad_in, grad_down[None]], axis=0))
+    return (out_part, dx_part, jnp.concatenate([pre_grad, hidden[None]], axis=0))
 
 
 def cold_terms(row_block, cold_in, cold_down):
@@ -77,6 +75,13 @@
         send_rows[:, :, None], (2, cold_count, 2, capacity, model_width)
     ).reshape(2, owner_count, capacity, model_width)
     received = lax.all_to_all(duplicate, "expert", split_axis=1, concat_axis=1, tiled=True)
+    full_stack = lax.all_gather(hot_stack, "dp", axis=1, tiled=True)
+    received, full_stack = lax.optimization_barrier((received, full_stack))
+    width = model_width // owner_count
+    by_column = jnp.stack([tokens, cotangent]).reshape(2, tok_dev, owner_count, width)
+    columns = lax.all_to_all(
+        by_column.transpose(0, 2, 1, 3), "expert", split_axis=1, concat_axis=1, tiled=True
+    ).reshape(2, owner_count * tok_dev, width)
     row_block = received.reshape(2, owner_count * capacity, model_width)
     out_part, dx_part, cold_grad_in, cold_grad_down = cold_terms(row_block, cold_in, cold_down)
     returned = lax.all_to_all(
@@ -86,22 +91,32 @@
         concat_axis=1,
         tiled=True,
     )
-    summed = jnp.sum(
-        returned.astype(jnp.float32).reshape(2, cold_count, 2, capacity, model_width), axis=2
+    pick = jnp.broadcast_to(
+        dispatch.reshape(-1, cold_count, 1, capacity), (dispatch.shape[0], cold_count, 2, capacity)
+    ).reshape(dispatch.shape[0], owner_count * capacity)
+    picked = jnp.einsum(
+        "rc,scd->srd",
+        pick,
+        returned.reshape(2, owner_count * capacity, model_width),
+        preferred_element_type=jnp.float32,
     )
-    summed = summed.reshape(2, cold_count * capacity, model_width)
-    picked = jnp.take(summed, column, axis=1)
     cold_out = jnp.sum(
         gates_flat.reshape(tok_dev, top_cold, 1)
         * picked[0].reshape(tok_dev, top_cold, model_width),
         axis=1,
     )
     cold_dx = jnp.sum(picked[1].reshape(tok_dev, top_cold, model_width), axis=1)
-    full_stack = lax.all_gather(hot_stack, "dp", axis=1, tiled=True)
-    hot_out, hot_dx, full_grads = hot_terms(tokens, cotangent, hot_weight, full_stack)
-    hot_grads = lax.psum_scatter(full_grads, "dp", scatter_dimension=1, tiled=True)
+    hot_out, hot_dx, unit_rows = hot_terms(tokens, cotangent, hot_weight, full_stack)
+    group_rows = lax.all_gather(unit_rows, "expert", axis=1, tiled=True)
+    group_in = jnp.einsum(
+        "ktu,td->kud", group_rows[:2], columns[0], preferred_element_type=jnp.float32
+    )
+    group_down = jnp.einsum(
+        "tu,td->ud", group_rows[2], columns[1], preferred_element_type=jnp.float32
+    )
+    group_grads = jnp.concatenate([group_in, group_down[None]], axis=0)
     scale_hot = 1.0 / math.sqrt(tok_dev * data_count * owner_count)
-    hot_cols = lax.psum_scatter(hot_grads, "expert", scatter_dimension=2, tiled=True) * scale_hot
+    hot_cols = lax.psum_scatter(group_grads, "dp", scatter_dimension=1, tiled=True) * scale_hot
     scale_cold = 1.0 / math.sqrt(tok_dev * owner_count)
     mixed = (hot_out + cold_out).astype(jnp.bfloat16)
     input_grad = (hot_dx + cold_dx).astype(jnp.bfloat16)

time: 370 us -> 277 us (0.75)
  waiting for transfers between devices: 279 us -> 184 us
  other arithmetic: 19.8 us -> 12.6 us
  starting transfers between devices: 11.1 us -> 16.4 us
    reduce_scatter x2 -> x1, waiting for transfers between devices: 133 us -> 11.9 us  [body(): lax.psum_scatter(group_grads, 'dp', scatter_dimension=1, tiled=True)]
    all_to_all x1, waiting for transfers between devices: 83.6 us -> 0.01 us  [body(): lax.all_to_all(jnp.stack([out_part, dx_part]).reshape(2, owner_count, cap...]
    all_gather x0 -> x1, waiting for transfers between devices: none -> 82 us  [body(): group_rows = lax.all_gather(unit_rows, 'expert', axis=1, tiled=True)]
    all_gather x1, waiting for transfers between devices: 62.6 us -> 0.01 us  [body(): full_stack = lax.all_gather(hot_stack, 'dp', axis=1, tiled=True)]
    all_to_all x1, waiting for transfers between devices: 0.01 us -> 59.5 us  [body(): lax.all_to_all(duplicate, 'expert', split_axis=1, concat_axis=1, tiled=True)]
    all_to_all x0 -> x1, waiting for transfers between devices: none -> 30.4 us  [body(): lax.all_to_all(by_column.transpose(0, 2, 1, 3), 'expert', split_axis=1, c...]
    gather x1 -> x0, local copies, waits for them, and re-layouts: 5.74 us -> none  [body(): picked = jnp.take(summed, column, axis=1)]
    all_to_all x0 -> x1, starting transfers between devices: none -> 4.25 us  [body(): lax.all_to_all(by_column.transpose(0, 2, 1, 3), 'expert', split_axis=1, c...]
  transfers between devices with their start and end apart: 5 -> 6, of which waited for: 4 -> 4; matrix products, arithmetic and copies ran while one was open for 11% -> 17% of each run, Pallas kernels for 0% -> 0%
where the time goes in v1:
time: 277 us; the launch traced here: 276 us
  waiting for transfers between devices  184 us (66%)
  matrix products  30.9 us (11%)
  local copies, waits for them, and re-layouts  18.2 us (7%)
  starting transfers between devices  16.4 us (6%)
  between operations  14.1 us (5%)
  other arithmetic  12.6 us (5%)
    all_gather x1, waiting for transfers between devices, body(): group_rows = lax.all_gather(unit_rows, 'expert', axis=1, tiled=True)  82 us
    all_to_all x1, waiting for transfers between devices, body(): lax.all_to_all(duplicate, 'expert', split_axis=1, concat_axis=1, tiled=True)  59.5 us
    all_to_all x1, waiting for transfers between devices, body(): lax.all_to_all(by_column.transpose(0, 2, 1, 3), 'expert', split_axis=1, c...  30.4 us
    reduce_scatter x1, waiting for transfers between devices, body(): lax.psum_scatter(group_grads, 'dp', scatter_dimension=1, tiled=True)  11.9 us
    all_to_all x1, starting transfers between devices, body(): lax.all_to_all(duplicate, 'expert', split_axis=1, concat_axis=1, tiled=True)  7.38 us
    unnamed x48, local copies, waits for them, and re-layouts  6.4 us
  transfers between devices with their start and end apart: 6, of which 4 were waited for; matrix products, arithmetic and copies ran while one was open for 17% of the time, Pallas kernels for 0%

profile of v1, /device:TPU:0, one launch (start us, length us, event | category | flops | bytes accessed | tf_op | source)
XLA Modules:
  0.0 276.0 jit_solution(17184605244955025126)
XLA Ops:
  7.2 3.3 %pad_maximum_fusion.1 = bf16[3,176,2048]{2,1,0:T(8,128)(2,1)} fusion(bf16[1,176,2048]{2,1,0:T(8,128)(2,1)} %bitcast.219, bf16[2,176,2048]{2,1,0:T(8,128)(2,1)} %param.16), kind=kLoop, calls=%fused_computation.24 | loop fusion | flops 1081344 | bytes 4325376 | tf_op jit(solution)/shard_map/concatenate | solution.py:55
  10.5 0.6 copy-done.13
  11.2 0.2 reduce_window_sum.11
  11.4 0.2 select_reduce_fusion
  11.6 1.2 fusion.39
  12.8 0.5 convolution_convert_fusion.1
  13.3 0.1 copy.24
  13.4 1.8 broadcast_in_dim.15
  15.2 7.4 %all-to-all-start = ((bf16[2,8,40,2048]{3,2,0,1:T(8,128)(2,1)}), bf16[2,8,40,2048]{3,2,0,1:T(8,128)(2,1)}, u32[]{:S(2)}, u32[]{:S(2)}) async-start(bf16[2,8,40,2048]{3,2,0,1:T(8,128)(2,1)} %bitcast.206), calls=%async_computation | async-start | bytes 5242880 | tf_op jit(solution)/shard_map/all_to_all | solution.py:77
  22.7 59.5 %all-to-all-done = bf16[2,8,40,2048]{3,2,0,1:T(8,128)(2,1)} async-done(((bf16[2,8,40,2048]{3,2,0,1:T(8,128)(2,1)}), bf16[2,8,40,2048]{3,2,0,1:T(8,128)(2,1)}, u32[]{:S(2)}, u32[]{:S(2)}) %all-to-all-start) | async-done | bytes 2621472 | tf_op jit(solution)/shard_map/all_to_all | solution.py:77
  82.2 4.5 %convolution_bitcast_fusion.3 = f32[2,128,704]{1,2,0:T(8,128)S(1)} fusion(bf16[3,704,2048]{2,1,0:T(8,128)(2,1)} %all-gather.3.cloned.1.call-done, bf16[128,2048]{1,0:T(8,128)(2,1)S(1)} %copy-done.1), kind=kOutput, calls=%fused_computation.29 | convolution fusion | flops 738197504 | bytes 9895936 | tf_op jit(solution)/shard_map/td,kud->ktu/dot_general | solution.py:15
  86.7 0.1 multiply_convert_fusion.4
  86.8 0.7 copy-done.8
  87.5 0.9 fusion.67
  88.5 0.7 copy-done.9
  89.2 0.9 pad_maximum_fusion.3
  90.1 2.0 copy.30
  92.2 1.0 copy.29
  93.2 2.3 maximum_bitcast_fusion
  95.4 2.3 copy.31
  97.7 4.2 %all-to-all-start.2 = ((bf16[2,8,128,256]{3,2,0,1:T(8,128)(2,1)}), bf16[2,8,128,256]{3,2,0,1:T(8,128)(2,1)}, u32[]{:S(2)}, u32[]{:S(2)}) async-start(bf16[2,8,128,256]{3,2,0,1:T(8,128)(2,1)} %copy.31), calls=%async_computation.2 | async-start | bytes 2097152 | tf_op jit(solution)/shard_map/all_to_all | solution.py:82
  102.0 1.9 fusion.79
  103.9 1.3 convolution_bitcast_fusion.2
  105.2 1.0 copy-done.15
  106.2 0.9 convolution_convert_fusion
  107.2 0.9 fusion.64
  108.1 1.2 fusion.8
  109.4 1.7 pad_maximum_fusion
  111.1 30.4 %all-to-all-done.2 = bf16[2,8,128,256]{3,2,0,1:T(8,128)(2,1)} async-done(((bf16[2,8,128,256]{3,2,0,1:T(8,128)(2,1)}), bf16[2,8,128,256]{3,2,0,1:T(8,128)(2,1)}, u32[]{:S(2)}, u32[]{:S(2)}) %all-to-all-start.2) | async-done | bytes 1048608 | tf_op jit(solution)/shard_map/all_to_all | solution.py:82
  141.5 4.4 %all-to-all-start.1 = ((bf16[2,8,40,2048]{3,2,0,1:T(8,128)(2,1)}), bf16[2,8,40,2048]{3,2,0,1:T(8,128)(2,1)}, u32[]{:S(2)}, u32[]{:S(2)}) async-start(bf16[2,8,40,2048]{3,2,0,1:T(8,128)(2,1)} %pad_maximum_fusion), calls=%async_computation.1 | async-start | bytes 5242880 | tf_op jit(solution)/shard_map/all_to_all | solution.py:87
  145.9 0.2 reduce-scatter.2.cloned.1.call-start
  146.1 2.1 fusion.80
  148.2 82.0 %all-gather.5.cloned.1.call-done = bf16[3,1024,704]{1,2,0:T(8,128)(2,1)} async-done(((bf16[3,128,704]{1,2,0:T(8,128)(2,1)}), bf16[3,1024,704]{1,2,0:T(8,128)(2,1)}) %all-gather.5.cloned.1.call-update) | async-done | bytes 4325392 | tf_op jit(solution)/shard_map/all_gather | solution.py:110
  230.2 2.0 fusion.28
  232.3 2.7 fusion.83
  235.0 1.5 pad_maximum_fusion.2
  236.5 0.1 compare_convert_fusion
  236.7 3.8 %fusion.9 = bf16[1,352,2048]{2,1,0:T(8,128)(2,1)} fusion(bf16[320,2048]{1,0:T(8,128)(2,1)} %bitcast.216, f32[2,320,352]{2,1,0:T(8,128)} %copy-done.18), kind=kOutput, calls=%fused_computation.16 | convolution fusion | flops 463491072 | bytes 3653632 | tf_op jit(solution)/shard_map/ru,rd->ud/dot_general | solution.py:41
  240.5 3.3 %fusion.2 = bf16[1,2,352,2048]{3,2,1,0:T(8,128)(2,1)} fusion(bf16[320,2048,1]{1,0,2:T(8,128)(2,1)S(1)} %bitcast.214, bf16[1,320,352]{2,1,0:T(8,128)(2,1)S(1)} %copy-done.22, bf16[1,320,352]{2,1,0:T(8,128)(2,1)S(1)} %copy-done.20), kind=kOutput, calls=%fused_computation.3 | convolution fusion | flops 925855744 | bytes 4644864 | tf_op jit(solution)/shard_map/kru,rd->kud/dot_general | solution.py:40
  243.8 2.2 copy.27
  246.0 0.8 convolution_bitcast_fusion.1
  246.8 0.1 copy-done.4
  246.9 3.3 %fusion.21 = bf16[128,2048]{1,0:T(8,128)(2,1)} fusion(bf16[3,704,2048]{2,1,0:T(8,128)(2,1)} %all-gather.3.cloned.1.call-done, f32[2,128,2048]{2,1,0:T(8,128)S(1)} %convolution_bitcast_fusion.1, f32[128]{0:T(128)S(1)} %bitcast.225, bf16[1,128,704]{1,2,0:T(8,128)(2,1)S(1)} %copy-done.4), kind=kOutput, calls=%fused_computation.22 | convolution fusion | flops 369885184 | bytes 4637184 | tf_op jit(solution)/shard_map/dot_general | solution.py:18
  250.2 4.8 %fusion.24 = bf16[128,2048]{1,0:T(8,128)(2,1)} fusion(bf16[3,704,2048]{2,1,0:T(8,128)(2,1)} %all-gather.3.cloned.1.call-done, f32[2,128,2048]{2,1,0:T(8,128)S(1)} %convolution_bitcast_fusion.1, bf16[1,128,704]{1,2,0:T(8,128)(2,1)S(1)} %copy-done.12, bf16[1,128,704]{1,2,0:T(8,128)(2,1)S(1)} %copy-done.10), kind=kOutput, calls=%fused_computation.23 | convolution fusion | flops 738902016 | bytes 7700480 | tf_op jit(solution)/shard_map/ktu,kud->td/dot_general | solution.py:24
  255.0 11.9 %reduce-scatter.2.cloned.1.call-done = f32[3,176,256]{2,1,0:T(8,128)} async-done(((f32[3,704,256]{2,1,0:T(8,128)}), f32[3,176,256]{2,1,0:T(8,128)}) %reduce-scatter.2.cloned.1.call-update) | async-done | bytes 540688 | tf_op jit(solution)/shard_map/reduce_scatter | solution.py:119
  266.9 1.1 broadcast_multiply_fusion
  268.0 0.8 slice.83
  268.8 0.7 slice_bitcast_fusion.6
  (53 shorter events, 0.5 us)
Async XLA Ops:
  7.2 96.7 %copy-start = (bf16[2,352,2048]{2,1,0:T(8,128)(2,1)S(1)}, bf16[2,352,2048]{2,1,0:T(8,128)(2,1)}, u32[]{:S(2)}) copy-start(bf16[2,352,2048]{2,1,0:T(8,128)(2,1)} %param.18) | copy-start | bytes 8650756
  7.2 75.0 %all-gather.3.cloned.1.call-start = ((), (), s32[]{:S(2)}) async-start(), calls=%async_computation.4 | async-start | bytes 10813440 | tf_op jit(solution)/shard_map/all_gather | solution.py:78
  10.5 0.7 copy-start.13
  10.5 1.1 copy-start.14
  10.5 2.3 copy-start.1
  15.2 7.4 %copy-start.16 = (f32[128]{0:T(128)S(1)}, f32[128]{0:T(128)}, u32[]{:S(2)}) copy-start(f32[128]{0:T(128)} %param.13) | copy-start | bytes 1540
  15.2 7.4 %copy-start.17 = (s32[128]{0:T(128)S(1)}, s32[128]{0:T(128)}, u32[]{:S(2)}) copy-start(s32[128]{0:T(128)} %param.12) | copy-start | bytes 1540
  15.2 67.0 %all-to-all-start = ((bf16[2,8,40,2048]{3,2,0,1:T(8,128)(2,1)}), bf16[2,8,40,2048]{3,2,0,1:T(8,128)(2,1)}, u32[]{:S(2)}, u32[]{:S(2)}) async-start(bf16[2,8,40,2048]{3,2,0,1:T(8,128)(2,1)} %bitcast.206), calls=%async_computation | async-start | bytes 5242880 | tf_op jit(solution)/shard_map/all_to_all | solution.py:77
  22.6 207.6 %all-gather.5.cloned.1.call-start = ((), (), s32[]{:S(2)}) async-start(), calls=%async_computation.5 | async-start | bytes 4866048 | tf_op jit(solution)/shard_map/all_gather | solution.py:110
  82.2 4.6 %copy-start.2 = (bf16[128,2048]{1,0:T(8,128)(2,1)S(1)}, bf16[128,2048]{1,0:T(8,128)(2,1)}, u32[]{:S(2)}) copy-start(bf16[128,2048]{1,0:T(8,128)(2,1)} %param.11) | copy-start | bytes 1572868
  82.2 5.3 %copy-start.8 = (bf16[3,704,2048]{2,1,0:T(8,128)(2,1)S(1)}, bf16[3,704,2048]{2,1,0:T(8,128)(2,1)}, u32[]{:S(2)}) copy-start(bf16[3,704,2048]{2,1,0:T(8,128)(2,1)} %all-gather.3.cloned.1.call-done) | copy-start | bytes 25952260
  87.5 1.0 copy-start.3
  88.5 0.7 copy-start.9
  88.5 0.8 copy-start.11
  97.7 43.7 %all-to-all-start.2 = ((bf16[2,8,128,256]{3,2,0,1:T(8,128)(2,1)}), bf16[2,8,128,256]{3,2,0,1:T(8,128)(2,1)}, u32[]{:S(2)}, u32[]{:S(2)}) async-start(bf16[2,8,128,256]{3,2,0,1:T(8,128)(2,1)} %copy.31), calls=%async_computation.2 | async-start | bytes 2097152 | tf_op jit(solution)/shard_map/all_to_all | solution.py:82
  103.9 1.3 copy-start.5
  103.9 3.2 %copy-start.7 = (bf16[1,8,40,2048]{3,2,0,1:T(8,128)(2,1)}, bf16[1,8,40,2048]{3,2,0,1:T(8,128)(2,1)S(1)}, u32[]{:S(2)}) copy-start(bf16[1,8,40,2048]{3,2,0,1:T(8,128)(2,1)S(1)} %get-tuple-element.11) | copy-start | bytes 3932164
  103.9 2.3 copy-start.15
  106.2 1.0 copy-start.18
  108.1 1.2 copy-start.19
  108.1 1.2 copy-start.21
  141.5 102.3 %all-to-all-start.1 = ((bf16[2,8,40,2048]{3,2,0,1:T(8,128)(2,1)}), bf16[2,8,40,2048]{3,2,0,1:T(8,128)(2,1)}, u32[]{:S(2)}, u32[]{:S(2)}) async-start(bf16[2,8,40,2048]{3,2,0,1:T(8,128)(2,1)} %pad_maximum_fusion), calls=%async_computation.1 | async-start | bytes 5242880 | tf_op jit(solution)/shard_map/all_to_all | solution.py:87
  145.9 121.0 %reduce-scatter.2.cloned.1.call-start = ((), (), s32[]{:S(2)}) async-start(), calls=%async_computation.6 | async-start | bytes 2703360 | tf_op jit(solution)/shard_map/reduce_scatter | solution.py:119
  236.6 3.9 %copy-start.6 = (bf16[1,8,40,2048]{3,2,0,1:T(8,128)(2,1)S(1)}, bf16[1,8,40,2048]{3,2,0,1:T(8,128)(2,1)}, u32[]{:S(2)}) copy-start(bf16[1,8,40,2048]{3,2,0,1:T(8,128)(2,1)} %copy-done.5) | copy-start | bytes 3932164
  236.6 3.8 %copy-start.20 = (bf16[1,320,352]{2,1,0:T(8,128)(2,1)S(1)}, bf16[1,320,352]{2,1,0:T(8,128)(2,1)}, u32[]{:S(2)}) copy-start(bf16[1,320,352]{2,1,0:T(8,128)(2,1)} %copy-done.19) | copy-start | bytes 675844
  236.7 3.8 %copy-start.22 = (bf16[1,320,352]{2,1,0:T(8,128)(2,1)S(1)}, bf16[1,320,352]{2,1,0:T(8,128)(2,1)}, u32[]{:S(2)}) copy-start(bf16[1,320,352]{2,1,0:T(8,128)(2,1)} %copy-done.21) | copy-start | bytes 675844
  246.0 0.9 copy-start.4
  246.9 3.3 %copy-start.10 = (bf16[1,128,704]{1,2,0:T(8,128)(2,1)S(1)}, bf16[1,128,704]{1,2,0:T(8,128)(2,1)}, u32[]{:S(2)}) copy-start(bf16[1,128,704]{1,2,0:T(8,128)(2,1)} %copy-done.9) | copy-start | bytes 540676
  246.9 3.3 %copy-start.12 = (bf16[1,128,704]{1,2,0:T(8,128)(2,1)S(1)}, bf16[1,128,704]{1,2,0:T(8,128)(2,1)}, u32[]{:S(2)}) copy-start(bf16[1,128,704]{1,2,0:T(8,128)(2,1)} %copy-done.11) | copy-start | bytes 540676
Sparse Core Ops, SparseCore 0:
  10.7 62.4 all-gather.2
  90.2 139.9 all-gather.4
  236.6 30.2 reduce-scatter.1
